TPU v7x, 32 devices: a whole 2x2x4 slice. The times are simulated.
32 devices in a mesh: dp: 4 (over y, x), expert: 4 (over z), tensor: 2 (over core).
Axes of the slice: x: 2, y: 2, z: 4, core: 2. Of those that a mesh axis runs over, the one named last changes fastest.
Arguments:
- tokens: bfloat16 [512, 6144], P('expert'), may hold values from -6 to 6
- routes: int32 [512, 2], P('expert'), may hold values from 0 to 3, all different within a row; in each aligned block of 128 rows (0 to 127, 128 to 255, ...) at most 128 rows name the same one
- logits: float32 [512, 2], P('expert'), may hold values from -8 to 8
- grad_out: bfloat16 [512, 6144], P('expert'), may hold values from -6 to 6
- w_gate: bfloat16 [4, 6144, 8192], P('expert', None, ('dp', 'tensor')), may hold values from -0.078125 to 0.078125
- w_up: bfloat16 [4, 6144, 8192], P('expert', None, ('dp', 'tensor')), may hold values from -0.078125 to 0.078125
- w_down: bfloat16 [4, 8192, 6144], P('expert', ('dp', 'tensor')), may hold values from -0.0625 to 0.0625
Outputs:
- output: bfloat16 [512, 6144], P(('expert', 'tensor'))
- grad_tokens: bfloat16 [512, 6144], P(('expert', 'tensor'))
Inputs may be any that keep to these rules, and one draw needn't show every extreme that they name: `routes`: each token names two different experts. The 128 tokens of one index of the expert axis name one expert at most 128 times, and in every draw some expert is named exactly 128 times by the tokens of some index.
All inputs are finite; a program needn't handle non-finite values.
Results may differ from a plain program's by a relative error of at most 0.015.
Values may be sent and summed in bfloat16 or wider, within the bound.
A program may use at most 128 MiB of HBM per device.

v0:
```python
import jax
import jax.numpy as jnp
from jax import lax
from jax.sharding import PartitionSpec as P


def slot_targets(routes, experts, capacity):
    flat = routes.reshape(-1)
    labels = jnp.arange(experts, dtype=jnp.int32)
    onehot = (flat[:, None] == labels[None, :]).astype(jnp.int32)
    before = jnp.cumsum(onehot, axis=0) - onehot
    slot = jnp.sum(before * onehot, axis=1)
    return (flat * capacity + slot).reshape(-1, 2)


def activate(gate, up):
    sig = jax.nn.sigmoid(gate)
    return (gate * sig * up).astype(jnp.bfloat16)


def backprop(grad_hidden, gate, up):
    sig = jax.nn.sigmoid(gate)
    grad_gate = (grad_hidden * up * sig * (1.0 + gate * (1.0 - sig))).astype(jnp.bfloat16)
    grad_up = (grad_hidden * gate * sig).astype(jnp.bfloat16)
    return (grad_gate, grad_up)


def local(tokens, routes, logits, grad_out, w_gate, w_up, w_down):
    experts = lax.axis_size("expert")
    lanes = lax.axis_size("dp")
    tensor_size = lax.axis_size("tensor")
    group = lanes * tensor_size
    count, width = tokens.shape
    capacity = 4 * count // experts
    gate_w = w_gate[0]
    up_w = w_up[0]
    down_w = w_down[0]
    inner = gate_w.shape[1]
    contract_last = (((1,), (1,)), ((), ()))
    target = slot_targets(routes, experts, capacity)
    share = jax.nn.sigmoid(logits[:, 0] - logits[:, 1])
    weight_one = share[:, None]
    weight_two = (1.0 - share)[:, None]
    grad_one = (weight_one * grad_out.astype(jnp.float32)).astype(jnp.bfloat16)
    grad_two = (weight_two * grad_out.astype(jnp.float32)).astype(jnp.bfloat16)

    def project_in(flat):
        gate = jnp.dot(flat, gate_w, preferred_element_type=jnp.float32)
        up = jnp.dot(flat, up_w, preferred_element_type=jnp.float32)
        return jnp.concatenate([gate, up], axis=1)

    def project_back(flat):
        return lax.dot_general(flat, down_w, contract_last, preferred_element_type=jnp.float32)

    portion = capacity // group
    offset = lax.axis_index(("dp", "tensor")) * portion
    places = (
        jnp.arange(experts, dtype=jnp.int32)[:, None] * capacity
        + offset
        + jnp.arange(portion, dtype=jnp.int32)[None, :]
    )
    build_places = places.reshape(-1)
    first = (build_places[:, None] == target[None, :, 0]).astype(jnp.bfloat16)
    second = (build_places[:, None] == target[None, :, 1]).astype(jnp.bfloat16)
    rows_fwd = jnp.dot(first + second, tokens, preferred_element_type=jnp.float32).astype(
        jnp.bfloat16
    )
    rows_bwd = jnp.dot(first, grad_one, preferred_element_type=jnp.float32)
    rows_bwd = (rows_bwd + jnp.dot(second, grad_two, preferred_element_type=jnp.float32)).astype(
        jnp.bfloat16
    )
    rows_fwd, rows_bwd = (rows_fwd, rows_bwd)
    shape = (experts, portion, width)
    got_fwd, got_bwd = (
        lax.all_to_all(rows_fwd.reshape(shape), "expert", split_axis=0, concat_axis=0, tiled=True),
        lax.all_to_all(rows_bwd.reshape(shape), "expert", split_axis=0, concat_axis=0, tiled=True),
    )

    def move_in(arrived, project):
        piece = lax.all_gather(arrived, ("dp", "tensor"), axis=1, tiled=True)
        result = project(piece.reshape(-1, width))
        spread = result.reshape(piece.shape[0], piece.shape[1], -1)
        return spread.reshape(-1, spread.shape[2])

    share_rows = count // tensor_size
    piece_rows = share_rows // lanes
    position = jnp.arange(count, dtype=jnp.int32)
    block_index = position // piece_rows
    within = position % piece_rows
    source = (
        block_index % tensor_size * share_rows + block_index // tensor_size * piece_rows + within
    )
    slot_one = target[source, 0]
    slot_two = target[source, 1]
    first_weight = weight_one[source]
    second_weight = weight_two[source]

    def settle(term, left_weight, right_weight):
        shaped = term.astype(jnp.bfloat16).reshape(experts, capacity, width)
        back = lax.all_to_all(shaped, "expert", split_axis=0, concat_axis=0, tiled=True).reshape(
            -1, width
        )
        mixed = left_weight * back[slot_one].astype(jnp.float32) + right_weight * back[
            slot_two
        ].astype(jnp.float32)
        mixed = lax.optimization_barrier(mixed.astype(jnp.bfloat16)).astype(jnp.float32)
        summed = lax.psum_scatter(
            mixed.astype(jnp.bfloat16), ("dp", "tensor"), scatter_dimension=0, tiled=True
        )
        return summed

    projected = move_in(got_fwd, project_in)
    gate = projected[:, :inner]
    up = projected[:, inner:]
    hidden = activate(gate, up)
    out_piece = settle(
        jnp.dot(hidden, down_w, preferred_element_type=jnp.float32), first_weight, second_weight
    )
    grad_hidden = move_in(got_bwd, project_back)
    grad_gate, grad_up = backprop(grad_hidden, gate, up)
    term = lax.dot_general(grad_gate, gate_w, contract_last, preferred_element_type=jnp.float32)
    term = term + lax.dot_general(grad_up, up_w, contract_last, preferred_element_type=jnp.float32)
    grad_piece = settle(term, 1.0, 1.0)
    output, grad_tokens = (
        lax.all_gather(out_piece, "dp", axis=0, tiled=True),
        lax.all_gather(grad_piece, "dp", axis=0, tiled=True),
    )
    return (output, grad_tokens)


def solution(mesh):
    return jax.shard_map(
        local,
        mesh=mesh,
        in_specs=(
            P("expert", None),
            P("expert", None),
            P("expert", None),
            P("expert", None),
            P("expert", None, ("dp", "tensor")),
            P("expert", None, ("dp", "tensor")),
            P("expert", ("dp", "tensor"), None),
        ),
        out_specs=(P(("expert", "tensor"), None), P(("expert", "tensor"), None)),
        check_vma=False,
    )
```

profile of v0, /device:TPU:0, one launch (start us, length us, event | category | flops | bytes accessed | tf_op | source)
XLA Modules:
  0.0 532.2 jit_solution(2563875377684586066)
XLA Ops:
  7.2 0.9 copy.11
  8.4 1.2 reduce-window.6
  11.6 26.5 %all_to_all.20 = bf16[4,16,6144]{2,1,0:T(8,128)(2,1)} all-to-all(bf16[4,16,6144]{2,1,0:T(8,128)(2,1)S(1)} %bitcast.76), channel_id=1, replica_groups=mesh['dp'=4,'expert'=4,'tensor'=2] {'expert'}, dimensions={0} | all-to-all | bytes 1572864 | tf_op jit(solution)/shard_map/all_to_all | solution.py:75
  39.3 22.4 %all_to_all.21 = bf16[4,16,6144]{2,1,0:T(8,128)(2,1)} all-to-all(bf16[4,16,6144]{2,1,0:T(8,128)(2,1)S(1)} %bitcast.75), channel_id=1, replica_groups=mesh['dp'=4,'expert'=4,'tensor'=2] {'expert'}, dimensions={0} | all-to-all | bytes 1572864 | tf_op jit(solution)/shard_map/all_to_all | solution.py:76
  61.7 21.2 %all-gather.3.cloned.1.call-done = bf16[4,128,6144]{2,1,0:T(8,128)(2,1)} async-done(((bf16[4,16,6144]{2,1,0:T(8,128)(2,1)}), bf16[4,128,6144]{2,1,0:T(8,128)(2,1)}) %all-gather.3.cloned.1.call-update) | async-done | bytes 6291472 | tf_op jit(solution)/shard_map/all_gather | solution.py:80
  82.9 14.2 %fusion.10 = f32[512,1024]{1,0:T(8,128)} fusion(bf16[512,6144]{1,0:T(8,128)(2,1)} %bitcast.78, bf16[1,6144,1024]{2,1,0:T(8,128)(2,1)} %param.11), kind=kOutput, calls=%fused_computation.18 | convolution fusion | flops 6442450944 | bytes 20971520 | tf_op jit(solution)/shard_map/dot_general | solution.py:48
  97.1 10.6 %fusion.6 = f32[512,1024]{1,0:T(8,128)} fusion(bf16[512,6144]{1,0:T(8,128)(2,1)S(1)} %bitcast.79, bf16[1,6144,1024]{2,1,0:T(8,128)(2,1)} %param.12), kind=kOutput, calls=%fused_computation.14 | convolution fusion | flops 6442450944 | bytes 20971520 | tf_op jit(solution)/shard_map/dot_general | solution.py:49
  107.7 22.6 %all-gather.5.cloned.1.call-done = bf16[4,128,6144]{2,1,0:T(8,128)(2,1)} async-done(((bf16[4,16,6144]{2,1,0:T(8,128)(2,1)}), bf16[4,128,6144]{2,1,0:T(8,128)(2,1)}) %all-gather.5.cloned.1.call-update) | async-done | bytes 6291472 | tf_op jit(solution)/shard_map/all_gather | solution.py:80
  130.3 11.7 %fusion = f32[512,1024]{1,0:T(8,128)S(1)} fusion(bf16[512,6144]{1,0:T(8,128)(2,1)} %bitcast.80, bf16[1,1024,6144]{2,1,0:T(8,128)(2,1)} %param.13), kind=kOutput, calls=%fused_computation.8 | convolution fusion | flops 6442450944 | bytes 20971520 | tf_op jit(solution)/shard_map/dot_general | solution.py:53
  142.0 1.3 copy-done.6
  143.3 14.2 %fusion.4 = f32[512,6144]{1,0:T(8,128)} fusion(bf16[1,6144,1024]{2,1,0:T(8,128)(2,1)} %param.12, f32[512,1024]{1,0:T(8,128)S(1)} %fusion, f32[512,1024]{1,0:T(8,128)S(1)} %copy-done.5), kind=kOutput, calls=%fused_computation.12 | convolution fusion | flops 6445596672 | bytes 29360128 | tf_op jit(solution)/shard_map/dot_general | solution.py:122
  157.5 16.1 %add_convert_fusion = bf16[512,6144]{1,0:T(8,128)(2,1)} fusion(f32[512,6144]{1,0:T(8,128)} %fusion.4, bf16[1,6144,1024]{2,1,0:T(8,128)(2,1)} %param.11, f32[512,1024]{1,0:T(8,128)} %fusion.10, f32[512,1024]{1,0:T(8,128)} %copy-done.6, f32[512,1024]{1,0:T(8,128)} %fusion.6), kind=kOutput, calls=%fused_computation.20 | convolution fusion | flops 6453985280 | bytes 37748736 | tf_op jit(solution)/shard_map/dot_general | solution.py:121
  173.6 5.2 all-to-all-start.3
  178.8 12.7 %fusion.14 = bf16[512,6144]{1,0:T(8,128)(2,1)} fusion(bf16[1,1024,6144]{2,1,0:T(8,128)(2,1)} %param.13, f32[512,1024]{1,0:T(8,128)} %fusion.6, f32[512,1024]{1,0:T(8,128)} %fusion.10), kind=kOutput, calls=%fused_computation.21 | convolution fusion | flops 6448742400 | bytes 23068672 | tf_op jit(solution)/shard_map/dot_general | solution.py:117
  191.5 126.1 %all-to-all-done.3 = bf16[4,128,6144]{2,1,0:T(8,128)(2,1)} async-done(((bf16[4,128,6144]{2,1,0:T(8,128)(2,1)}), bf16[4,128,6144]{2,1,0:T(8,128)(2,1)}, u32[]{:S(2)}, u32[]{:S(2)}) %all-to-all-start.3) | async-done | bytes 6291488 | tf_op jit(solution)/shard_map/all_to_all | solution.py:100
  317.6 5.2 all-to-all-start.1
  323.0 1.7 gather_fusion.1
  324.8 1.5 gather_fusion.4
  326.3 6.6 %gather_fusion.6 = bf16[128,6144]{1,0:T(8,128)(2,1)S(1)} fusion(bf16[512,6144]{1,0:T(8,128)(2,1)} %bitcast.23, s32[1024]{0:T(1024)S(1)} %pad_clamp_fusion.1), kind=kCustom, calls=%fused_computation.6 | custom fusion | bytes 3146240 | tf_op jit(solution)/shard_map/gather | solution.py:103
  332.9 7.8 %gather_fusion.7 = bf16[128,6144]{1,0:T(8,128)(2,1)} fusion(bf16[512,6144]{1,0:T(8,128)(2,1)} %bitcast.23, s32[1024]{0:T(1024)S(1)} %pad_clamp_fusion), kind=kCustom, calls=%fused_computation.7 | custom fusion | bytes 3146240 | tf_op jit(solution)/shard_map/gather | solution.py:103
  340.7 3.0 add_convert_fusion.1
  343.8 1.5 gather_fusion
  345.3 1.2 gather_fusion.3
  346.5 114.4 %all-to-all-done.1 = bf16[4,128,6144]{2,1,0:T(8,128)(2,1)} async-done(((bf16[4,128,6144]{2,1,0:T(8,128)(2,1)}), bf16[4,128,6144]{2,1,0:T(8,128)(2,1)}, u32[]{:S(2)}, u32[]{:S(2)}) %all-to-all-start.1) | async-done | bytes 6291488 | tf_op jit(solution)/shard_map/all_to_all | solution.py:100
  460.9 6.6 %gather_fusion.2 = bf16[128,6144]{1,0:T(8,128)(2,1)S(1)} fusion(bf16[512,6144]{1,0:T(8,128)(2,1)} %bitcast.12, s32[1024]{0:T(1024)S(1)} %pad_clamp_fusion.1), kind=kCustom, calls=%fused_computation.2 | custom fusion | bytes 3146240 | tf_op jit(solution)/shard_map/gather | solution.py:103
  467.5 6.6 %gather_fusion.5 = bf16[128,6144]{1,0:T(8,128)(2,1)S(1)} fusion(bf16[512,6144]{1,0:T(8,128)(2,1)} %bitcast.12, s32[1024]{0:T(1024)S(1)} %pad_clamp_fusion), kind=kCustom, calls=%fused_computation.5 | custom fusion | bytes 3146240 | tf_op jit(solution)/shard_map/gather | solution.py:103
  474.1 1.8 add_convert_fusion.2
  476.0 11.3 %all_gather.15 = bf16[64,6144]{1,0:T(8,128)(2,1)S(1)} all-gather(bf16[16,6144]{1,0:T(8,128)(2,1)} %reduce-scatter.5.cloned.1.call-done), channel_id=1, replica_groups=mesh['dp'=4,'expert'=4,'tensor'=2] {'dp'}, dimensions={0}, use_global_device_ids=true | all-gather | bytes 983040 | tf_op jit(solution)/shard_map/all_gather | solution.py:126
  487.3 25.5 %reduce-scatter.3.cloned.1.call-done = bf16[16,6144]{1,0:T(8,128)(2,1)} async-done(((bf16[128,6144]{1,0:T(8,128)(2,1)}), bf16[16,6144]{1,0:T(8,128)(2,1)}) %reduce-scatter.3.cloned.1.call-update) | async-done | bytes 196624 | tf_op jit(solution)/shard_map/reduce_scatter | solution.py:107
  512.8 11.1 %all_gather.13 = bf16[64,6144]{1,0:T(8,128)(2,1)S(1)} all-gather(bf16[16,6144]{1,0:T(8,128)(2,1)} %reduce-scatter.3.cloned.1.call-done), channel_id=1, replica_groups=mesh['dp'=4,'expert'=4,'tensor'=2] {'dp'}, dimensions={0}, use_global_device_ids=true | all-gather | bytes 983040 | tf_op jit(solution)/shard_map/all_gather | solution.py:125
  523.9 0.9 copy.20
  524.8 0.9 copy.21
  (51 shorter events, 3.7 us)
Async XLA Ops:
  7.2 4.0 copy-start
  7.2 75.7 %all-gather.3.cloned.1.call-start = ((), (), s32[]{:S(2)}) async-start(), calls=%async_computation.6 | async-start | bytes 7077888 | tf_op jit(solution)/shard_map/all_gather | solution.py:80
  11.1 27.0 %copy-start.3 = (f32[128,2]{0,1:T(2,128)S(1)}, f32[128,2]{0,1:T(2,128)}, u32[]{:S(2)}) copy-start(f32[128,2]{0,1:T(2,128)} %param.9) | copy-start | bytes 3076
  11.2 27.0 %copy-start.2 = (bf16[128,6144]{1,0:T(8,128)(2,1)S(1)}, bf16[128,6144]{1,0:T(8,128)(2,1)}, u32[]{:S(2)}) copy-start(bf16[128,6144]{1,0:T(8,128)(2,1)} %param.10) | copy-start | bytes 4718596
  38.1 92.3 %all-gather.5.cloned.1.call-start = ((), (), s32[]{:S(2)}) async-start(), calls=%async_computation.8 | async-start | bytes 7077888 | tf_op jit(solution)/shard_map/all_gather | solution.py:80
  82.9 14.2 %copy-start.4 = (bf16[4,128,6144]{2,1,0:T(8,128)(2,1)S(1)}, bf16[4,128,6144]{2,1,0:T(8,128)(2,1)}, u32[]{:S(2)}) copy-start(bf16[4,128,6144]{2,1,0:T(8,128)(2,1)} %all-gather.3.cloned.1.call-done) | copy-start | bytes 18874372
  130.3 13.0 %copy-start.5 = (f32[512,1024]{1,0:T(8,128)S(1)}, f32[512,1024]{1,0:T(8,128)}, u32[]{:S(2)}) copy-start(f32[512,1024]{1,0:T(8,128)} %fusion.10) | copy-start | bytes 6291460
  142.0 1.3 copy-start.6
  173.6 144.1 %all-to-all-start.3 = ((bf16[4,128,6144]{2,1,0:T(8,128)(2,1)}), bf16[4,128,6144]{2,1,0:T(8,128)(2,1)}, u32[]{:S(2)}, u32[]{:S(2)}) async-start(bf16[4,128,6144]{2,1,0:T(8,128)(2,1)} %bitcast.74), calls=%async_computation.4 | async-start | bytes 12582912 | tf_op jit(solution)/shard_map/all_to_all | solution.py:100
  317.6 143.3 %all-to-all-start.1 = ((bf16[4,128,6144]{2,1,0:T(8,128)(2,1)}), bf16[4,128,6144]{2,1,0:T(8,128)(2,1)}, u32[]{:S(2)}, u32[]{:S(2)}) async-start(bf16[4,128,6144]{2,1,0:T(8,128)(2,1)} %bitcast.73), calls=%async_computation.1 | async-start | bytes 12582912 | tf_op jit(solution)/shard_map/all_to_all | solution.py:100
  322.9 153.1 %reduce-scatter.5.cloned.1.call-start = ((), (), s32[]{:S(2)}) async-start(), calls=%async_computation.9 | async-start | bytes 1769472 | tf_op jit(solution)/shard_map/reduce_scatter | solution.py:107
  343.7 169.1 %reduce-scatter.3.cloned.1.call-start = ((), (), s32[]{:S(2)}) async-start(), calls=%async_computation.7 | async-start | bytes 1769472 | tf_op jit(solution)/shard_map/reduce_scatter | solution.py:107
  476.0 49.6 %copy-start.1 = (bf16[128,6144]{1,0:T(8,128)(2,1)S(1)}, bf16[128,6144]{1,0:T(8,128)(2,1)}, u32[]{:S(2)}) copy-start(bf16[128,6144]{1,0:T(8,128)(2,1)} %param.7) | copy-start | bytes 4718596
Sparse Core Ops, SparseCore 0:
  38.2 44.6 all-gather.2
  84.8 45.5 all-gather.4
  343.8 38.9 reduce-scatter.4
  476.1 36.6 reduce-scatter.2
where the time goes:
time: 533 us; the launch traced here: 532 us
  waiting for transfers between devices  310 us (58%)
  matrix products  80.9 us (15%)
  blocking collectives  71.2 us (13%)
  local copies, waits for them, and re-layouts  38.4 us (7%)
  between operations  14 us (3%)
  starting transfers between devices  10.7 us (2%)
  other arithmetic  7.04 us (1%)
    all_to_all x2, waiting for transfers between devices, settle(): lax.all_to_all(shaped, 'expert', split_axis=0, concat_axis=0, tiled=True)  241 us
    all_gather x2, waiting for transfers between devices, move_in(): piece = lax.all_gather(arrived, ('dp', 'tensor'), axis=1, tiled=True)  43.8 us
    all_to_all x1, blocking collectives, local(): lax.all_to_all(rows_fwd.reshape(shape), 'expert', split_axis=0, concat_ax...  26.5 us
    reduce_scatter x2, waiting for transfers between devices, settle(): lax.psum_scatter(mixed.astype(jnp.bfloat16), ('dp', 'tensor'), scatter_di...  25.5 us
    all_to_all x1, blocking collectives, local(): lax.all_to_all(rows_bwd.reshape(shape), 'expert', split_axis=0, concat_ax...  22.4 us
    dot_general x1, matrix products, local(): lax.dot_general(grad_gate, gate_w, contract_last, preferred_element_type=...  16.1 us
    gather x2, local copies, waits for them, and re-layouts, settle(): back[slot_two].astype(jnp.float32)  14.4 us
    dot_general x1, matrix products, project_in(): gate = jnp.dot(flat, gate_w, preferred_element_type=jnp.float32)  14.2 us
  transfers between devices with their start and end apart: 6, of which 5 were waited for; matrix products, arithmetic and copies ran while one was open for 14% of the time, Pallas kernels for 0%

commit v1 on v0

v1 whole, which is shorter than its diff:
```python
import functools

import jax
import jax.numpy as jnp
from jax import lax
from jax.experimental import pallas as pl
from jax.experimental.pallas import tpu as pltpu
from jax.sharding import PartitionSpec as P

MESH = pl.DeviceIdType.MESH
CONTRACT_LAST = (((1,), (1,)), ((), ()))
TILE = 256


def flip(index, mask):
    out = index
    bit = 1
    while bit <= mask:
        if mask & bit:
            out = out + bit - 2 * bit * lax.rem(index // bit, 2)
        bit *= 2
    return out


def expert_kernel(
    sizes,
    tokens,
    grads,
    table,
    w_gate,
    w_up,
    w_down,
    out_hbm,
    back_hbm,
    x_buf,
    g_buf,
    wg_buf,
    wu_buf,
    wd_buf,
    gate,
    up,
    gh,
    hid,
    gu,
    share_rows,
    share_cols,
    pair_buf,
    plane_buf,
    axis_buf,
    final_buf,
    w_sem,
    own_sem,
    t_send,
    t_recv,
    d1_send,
    d1_recv,
    d2_send,
    d2_recv,
    d3_send,
    d3_recv,
    r1_send,
    r1_recv,
    r2_send,
    r2_recv,
    r3_send,
    r3_recv,
    r4_send,
    r4_recv,
):
    lanes, experts, tensor = sizes
    i = lax.axis_index("dp")
    z = lax.axis_index("expert")
    t = lax.axis_index("tensor")
    count, width = tokens.shape
    inner = gate.shape[1]
    total = experts * count
    rows = count // tensor
    cols = width // lanes
    tile_f = min(TILE, inner)
    bufs = (x_buf, g_buf)

    def zz(k):
        return lax.rem(z + k, experts)

    def tt(s):
        return lax.rem(t + s, tensor)

    def row_ds(which):
        return pl.ds(pl.multiple_of(which * rows, rows), rows)

    def col_ds(which):
        return pl.ds(pl.multiple_of(which * cols, cols), cols)

    def remote(src, dst, send, recv, axis, target):
        return pltpu.make_async_remote_copy(
            src_ref=src,
            dst_ref=dst,
            send_sem=send,
            recv_sem=recv,
            device_id={axis: target},
            device_id_type=MESH,
        )

    def load(kind, m, slot):
        block = col_ds(flip(i, m))
        if kind == 0:
            pair = (w_gate.at[block, :], wg_buf.at[slot])
        elif kind == 1:
            pair = (w_up.at[block, :], wu_buf.at[slot])
        else:
            pair = (w_down.at[:, block], wd_buf.at[slot])
        return pltpu.make_async_copy(*pair, w_sem.at[kind, slot])

    loads = {}

    def fetch(kind, m, slot):
        loads[kind, slot] = load(kind, m, slot)
        loads[kind, slot].start()

    def fetched(kind, slot):
        copy = loads.pop((kind, slot), None)
        if copy is not None:
            copy.wait()

    own = [
        pltpu.make_async_copy(tokens, x_buf.at[z], own_sem.at[0]),
        pltpu.make_async_copy(grads, g_buf.at[z], own_sem.at[1]),
        pltpu.make_async_copy(table.at[z], share_rows.at[z], own_sem.at[2]),
    ]

    barrier = pltpu.get_barrier_semaphore()
    for k in range(1, experts):
        pl.semaphore_signal(barrier, inc=1, device_id={"expert": zz(k)}, device_id_type=MESH)
    for m in range(1, lanes):
        pl.semaphore_signal(barrier, inc=1, device_id={"dp": flip(i, m)}, device_id_type=MESH)
    for s in range(1, tensor):
        pl.semaphore_signal(barrier, inc=1, device_id={"tensor": tt(s)}, device_id_type=MESH)
    pl.semaphore_wait(barrier, experts + lanes + tensor - 3)

    def step_one(a):
        copies = []
        source = (tokens, grads)[a]
        for k in range(1, experts):
            copies.append(
                remote(
                    source.at[row_ds(t), col_ds(i)],
                    bufs[a].at[z, row_ds(t), col_ds(i)],
                    d1_send.at[a, k],
                    d1_recv.at[a, k],
                    "expert",
                    zz(k),
                )
            )
        for copy in copies:
            copy.start()
        return copies

    def step_two(a, k):
        copies = []
        place = bufs[a].at[zz(experts - k), row_ds(t), col_ds(i)]
        for m in range(1, lanes):
            copies.append(
                remote(place, place, d2_send.at[a, k, m], d2_recv.at[a, k, m], "dp", flip(i, m))
            )
        for copy in copies:
            copy.start()
        return copies

    def step_three(a, k, m):
        copies = []
        place = bufs[a].at[zz(experts - k), row_ds(t), col_ds(flip(i, m))]
        for s in range(1, tensor):
            copies.append(
                remote(
                    place, place, d3_send.at[a, k, m, s], d3_recv.at[a, k, m, s], "tensor", tt(s)
                )
            )
        for copy in copies:
            copy.start()
        return copies

    first = {0: step_one(0)}
    shares = []
    for k in range(1, experts):
        shares.append(
            remote(
                table.at[zz(k)],
                share_rows.at[z],
                t_send.at[k],
                t_recv.at[k],
                "expert",
                zz(k),
            )
        )
    for copy in shares:
        copy.start()
    for copy in own:
        copy.start()
    for slot in range(2):
        fetch(0, slot, slot)
        fetch(1, slot, slot)
    for slot in range(2):
        fetch(2, lanes - 1 - slot, slot)

    second = {}
    third = {}

    def relay_one(a):
        for k in range(1, experts):
            first[a][k - 1].wait_recv()
            second[a, k] = step_two(a, k)
            third[a, k, 0] = step_three(a, k, 0)

    def relay_two(a, m):
        for k in range(1, experts):
            second[a, k][m - 1].wait_recv()
            third[a, k, m] = step_three(a, k, m)

    def arrived(a, m):
        for k in range(1, experts):
            for copy in third[a, k, m]:
                copy.wait_recv()

    def sent(a):
        for copy in first[a]:
            copy.wait_send()
        for k in range(1, experts):
            for copy in second[a, k]:
                copy.wait_send()
            for m in range(lanes):
                for copy in third[a, k, m]:
                    copy.wait_send()

    def operand(a, m):
        return bufs[a][:, :, col_ds(flip(i, m))].reshape(total, cols)

    relay_one(0)
    first[1] = step_one(1)
    own[0].wait()
    for m in range(lanes):
        if m + 1 < lanes:
            relay_two(0, m + 1)
        else:
            relay_one(1)
        arrived(0, m)
        slot = m % 2
        fetched(0, slot)
        fetched(1, slot)

        def project(n, carry, m=m, slot=slot):
            span = pl.ds(pl.multiple_of(n * tile_f, tile_f), tile_f)
            left = operand(0, m)
            one = jnp.dot(left, wg_buf[slot, :, span], preferred_element_type=jnp.float32)
            two = jnp.dot(left, wu_buf[slot, :, span], preferred_element_type=jnp.float32)
            if m == 0:
                gate[:, span] = one
                up[:, span] = two
            else:
                gate[:, span] += one
                up[:, span] += two
            return carry

        lax.fori_loop(0, inner // tile_f, project, 0)
        if m + 2 < lanes:
            fetch(0, m + 2, slot)
            fetch(1, m + 2, slot)

    own[2].wait()
    for copy in shares:
        copy.wait()
    for e in range(experts):
        share_cols[e * count : (e + 1) * count, :] = jnp.broadcast_to(
            share_rows[e, 0:1, :], (count, count)
        ).T

    def activate(e, carry):
        span = pl.ds(pl.multiple_of(e * count, count), count)
        weight = share_cols[span, 0:1]
        for f in range(0, inner, tile_f):
            v = gate[span, f : f + tile_f]
            sig = jax.nn.sigmoid(v)
            hid[span, f : f + tile_f] = (v * sig * up[span, f : f + tile_f] * weight).astype(
                jnp.bfloat16
            )
        return carry

    lax.fori_loop(0, experts, activate, 0)
    sent(0)

    pairs = {}
    planes = {}

    def pair_send(a, m):
        copies = []
        for s in range(1, tensor):
            copies.append(
                remote(
                    bufs[a].at[:, row_ds(tt(s)), col_ds(flip(i, m))],
                    pair_buf.at[a, m, s - 1],
                    r1_send.at[a, m, s],
                    r1_recv.at[a, m, s],
                    "tensor",
                    tt(s),
                )
            )
        for copy in copies:
            copy.start()
        pairs[a, m] = copies

    def pair_sum(a, m):
        for copy in pairs[a, m]:
            copy.wait_recv()
        block = col_ds(flip(i, m))

        def add(e, carry):
            value = bufs[a][e, row_ds(t), block].astype(jnp.float32)
            for s in range(tensor - 1):
                value = value + pair_buf[a, m, s, e].astype(jnp.float32)
            bufs[a][e, row_ds(t), block] = value.astype(jnp.bfloat16)
            return carry

        lax.fori_loop(0, experts, add, 0)
        if m == 0:
            return
        for k in list(range(1, experts)) + [0]:
            copy = remote(
                bufs[a].at[zz(k), row_ds(t), block],
                plane_buf.at[a, m - 1, zz(k)],
                r2_send.at[a, m, k],
                r2_recv.at[a, m, k],
                "dp",
                flip(i, m),
            )
            copy.start()
            planes[a, m, k] = copy

    for n in range(lanes):
        m = lanes - 1 - n
        slot = n % 2
        fetched(2, slot)

        def down(c, carry, m=m, slot=slot):
            span = pl.ds(pl.multiple_of(c * TILE, TILE), TILE)
            to = pl.ds(pl.multiple_of(flip(i, m) * cols + c * TILE, TILE), TILE)
            value = jnp.dot(hid[...], wd_buf[slot, :, span], preferred_element_type=jnp.float32)
            x_buf[:, :, to] = value.astype(jnp.bfloat16).reshape(experts, count, TILE)
            return carry

        lax.fori_loop(0, cols // TILE, down, 0)
        if n + 2 < lanes:
            fetch(2, lanes - 1 - (n + 2), slot)
        pair_send(0, m)
        if n > 0:
            pair_sum(0, m + 1)
    relay_two(1, 1)
    pair_sum(0, 0)

    own[1].wait()
    for m in range(lanes):
        if 1 <= m < lanes - 1:
            relay_two(1, m + 1)
        arrived(1, m)
        slot = (lanes - 1 - m) % 2
        fetched(2, slot)

        def project_back(n, carry, m=m, slot=slot):
            span = pl.ds(pl.multiple_of(n * tile_f, tile_f), tile_f)
            value = lax.dot_general(
                operand(1, m),
                wd_buf[slot, span, :],
                CONTRACT_LAST,
                preferred_element_type=jnp.float32,
            )
            if m == 0:
                gh[:, span] = value
            else:
                gh[:, span] += value
            return carry

        lax.fori_loop(0, inner // tile_f, project_back, 0)
        if m + 2 < lanes:
            fetch(2, m + 2, slot)

    def differentiate(e, carry):
        span = pl.ds(pl.multiple_of(e * count, count), count)
        weight = share_cols[span, 0:1]
        for f in range(0, inner, tile_f):
            part = slice(f, f + tile_f)
            v = gate[span, part]
            sig = jax.nn.sigmoid(v)
            slope = gh[span, part] * weight * sig
            hid[span, part] = (slope * up[span, part] * (1.0 + v * (1.0 - sig))).astype(
                jnp.bfloat16
            )
            gu[span, part] = (slope * v).astype(jnp.bfloat16)
        return carry

    lax.fori_loop(0, experts, differentiate, 0)
    sent(1)

    for n in range(lanes):
        m = lanes - 1 - n
        slot = m % 2
        fetched(0, slot)
        fetched(1, slot)

        def back(c, carry, m=m, slot=slot):
            span = pl.ds(pl.multiple_of(c * TILE, TILE), TILE)
            to = pl.ds(pl.multiple_of(flip(i, m) * cols + c * TILE, TILE), TILE)
            value = lax.dot_general(
                hid[...], wg_buf[slot, span, :], CONTRACT_LAST, preferred_element_type=jnp.float32
            )
            value = value + lax.dot_general(
                gu[...], wu_buf[slot, span, :], CONTRACT_LAST, preferred_element_type=jnp.float32
            )
            g_buf[:, :, to] = value.astype(jnp.bfloat16).reshape(experts, count, TILE)
            return carry

        lax.fori_loop(0, cols // TILE, back, 0)
        if n + 2 < lanes:
            fetch(0, m - 2, slot)
            fetch(1, m - 2, slot)
        pair_send(1, m)
        if n > 0:
            pair_sum(1, m + 1)
    pair_sum(1, 0)

    crossing = {}
    for a in range(2):
        for k in list(range(1, experts)) + [0]:
            for m in range(1, lanes):
                planes[a, m, k].wait_recv()
            place = bufs[a].at[zz(k), row_ds(t), col_ds(i)]
            value = place[...].astype(jnp.float32)
            for m in range(1, lanes):
                value = value + plane_buf[a, m - 1, zz(k)].astype(jnp.float32)
            place[...] = value.astype(jnp.bfloat16)
            if k > 0:
                copy = remote(
                    place,
                    axis_buf.at[a, k - 1],
                    r3_send.at[a, k],
                    r3_recv.at[a, k],
                    "expert",
                    zz(k),
                )
                copy.start()
                crossing[a, k] = copy
    finals = []
    for a in range(2):
        value = bufs[a][z, row_ds(t), col_ds(i)].astype(jnp.float32)
        for k in range(1, experts):
            crossing[a, k].wait_recv()
            value = value + axis_buf[a, k - 1].astype(jnp.float32)
        final_buf[a] = value.astype(jnp.bfloat16)
        target = (out_hbm, back_hbm)[a].at[:, col_ds(i)]
        for m in range(1, lanes):
            finals.append(
                remote(
                    final_buf.at[a], target, r4_send.at[a, m], r4_recv.at[a, m], "dp", flip(i, m)
                )
            )
        finals.append(pltpu.make_async_copy(final_buf.at[a], target, own_sem.at[3 + a]))
        for copy in finals[-lanes:]:
            copy.start()
    for copies in pairs.values():
        for copy in copies:
            copy.wait_send()
    for copy in planes.values():
        copy.wait_send()
    for copy in crossing.values():
        copy.wait_send()
    for copy in finals:
        copy.wait()


def local(sizes, tokens, routes, logits, grad_out, w_gate, w_up, w_down):
    lanes, experts, tensor = sizes
    count, width = tokens.shape
    inner = w_gate.shape[2]
    rows = count // tensor
    cols = width // lanes
    total = experts * count
    share = jax.nn.sigmoid(logits[:, 0] - logits[:, 1])
    labels = jnp.arange(experts, dtype=jnp.int32)[:, None]
    table = jnp.where(routes[None, :, 0] == labels, share[None, :], 0.0)
    table = table + jnp.where(routes[None, :, 1] == labels, 1.0 - share[None, :], 0.0)
    table = jnp.broadcast_to(table[:, None, :], (experts, 8, count))
    bf16 = jnp.bfloat16
    f32 = jnp.float32
    dma = pltpu.SemaphoreType.DMA
    result = jax.ShapeDtypeStruct((rows, width), bf16)
    anywhere = pl.BlockSpec(memory_space=pl.ANY)
    flops = 2 * total * width * inner * 6
    return pl.pallas_call(
        functools.partial(expert_kernel, sizes),
        out_shape=(result, result),
        in_specs=[anywhere] * 6,
        out_specs=(anywhere, anywhere),
        scratch_shapes=[
            pltpu.VMEM((experts, count, width), bf16),
            pltpu.VMEM((experts, count, width), bf16),
            pltpu.VMEM((2, cols, inner), bf16),
            pltpu.VMEM((2, cols, inner), bf16),
            pltpu.VMEM((2, inner, cols), bf16),
            pltpu.VMEM((total, inner), f32),
            pltpu.VMEM((total, inner), f32),
            pltpu.VMEM((total, inner), f32),
            pltpu.VMEM((total, inner), bf16),
            pltpu.VMEM((total, inner), bf16),
            pltpu.VMEM((experts, 8, count), f32),
            pltpu.VMEM((total, count), f32),
            pltpu.VMEM((2, lanes, tensor - 1, experts, rows, cols), bf16),
            pltpu.VMEM((2, lanes - 1, experts, rows, cols), bf16),
            pltpu.VMEM((2, experts - 1, rows, cols), bf16),
            pltpu.VMEM((2, rows, cols), bf16),
            dma((3, 2)),
            dma((5,)),
            dma((experts,)),
            dma((experts,)),
            dma((2, experts)),
            dma((2, experts)),
            dma((2, experts, lanes)),
            dma((2, experts, lanes)),
            dma((2, experts, lanes, tensor)),
            dma((2, experts, lanes, tensor)),
            dma((2, lanes, tensor)),
            dma((2, lanes, tensor)),
            dma((2, lanes, experts)),
            dma((2, lanes, experts)),
            dma((2, experts)),
            dma((2, experts)),
            dma((2, lanes)),
            dma((2, lanes)),
        ],
        compiler_params=pltpu.CompilerParams(
            collective_id=0, has_side_effects=True, vmem_limit_bytes=62 * 1024 * 1024
        ),
        cost_estimate=pl.CostEstimate(
            flops=flops, bytes_accessed=6 * width * inner * 2, transcendentals=2 * total * inner
        ),
        name="expert_layer",
    )(tokens, grad_out, table, w_gate[0], w_up[0], w_down[0])


def solution(mesh):
    sizes = (mesh.shape["dp"], mesh.shape["expert"], mesh.shape["tensor"])
    return jax.shard_map(
        functools.partial(local, sizes),
        mesh=mesh,
        in_specs=(
            P("expert", None),
            P("expert", None),
            P("expert", None),
            P("expert", None),
            P("expert", None, ("dp", "tensor")),
            P("expert", None, ("dp", "tensor")),
            P("expert", ("dp", "tensor"), None),
        ),
        out_specs=(P(("expert", "tensor"), None), P(("expert", "tensor"), None)),
        check_vma=False,
    )
```

time: 533 us -> 176 us (0.33)
  waiting for transfers between devices: 310 us -> 0 us
  Pallas kernels: 0 us -> 168 us
  matrix products: 80.9 us -> 0 us
  blocking collectives: 71.2 us -> 0 us
  local copies, waits for them, and re-layouts: 38.4 us -> 5.5 us
  between operations: 14 us -> 0.64 us
  starting transfers between devices: 10.7 us -> 0 us
  other arithmetic: 7.04 us -> 0.77 us
    all_to_all x2 -> x0, waiting for transfers between devices: 241 us -> none  [settle(): lax.all_to_all(shaped, 'expert', split_axis=0, concat_axis=0, tiled=True)]
    pallas_call x0 -> x1, Pallas kernels: none -> 168 us  [local(): pl.pallas_call(functools.partial(expert_kernel, sizes), out_shape=(result...]
    dot_general x9 -> x0, matrix products: 80.9 us -> none  [the longest x1 16.1 us: local(): lax.dot_general(grad_gate, gate_w, contract_last, preferred_element_type=...]
    all_to_all x2 -> x0, blocking collectives: 48.8 us -> none  [the longest x1 26.5 us: local(): lax.all_to_all(rows_fwd.reshape(shape), 'expert', split_axis=0, concat_ax...]
    all_gather x2 -> x0, waiting for transfers between devices: 43.8 us -> none  [move_in(): piece = lax.all_gather(arrived, ('dp', 'tensor'), axis=1, tiled=True)]
    gather x8 -> x0, local copies, waits for them, and re-layouts: 33.5 us -> none  [the longest x2 14.4 us: settle(): back[slot_two].astype(jnp.float32)]
    reduce_scatter x2 -> x0, waiting for transfers between devices: 25.5 us -> none  [settle(): lax.psum_scatter(mixed.astype(jnp.bfloat16), ('dp', 'tensor'), scatter_di...]
    all_gather x2 -> x0, blocking collectives: 22.4 us -> none  [the longest x1 11.3 us: local(): lax.all_gather(grad_piece, 'dp', axis=0, tiled=True)]
  transfers between devices with their start and end apart: 6 -> 0, of which waited for: 5 -> 0; matrix products, arithmetic and copies ran while one was open for 14% -> 0% of each run, Pallas kernels for 0% -> 0%
where the time goes in v1:
time: 176 us; the launch traced here: 175 us
  Pallas kernels  168 us (95%)
  local copies, waits for them, and re-layouts  5.5 us (3%)
    pallas_call x1, Pallas kernels, local(): pl.pallas_call(functools.partial(expert_kernel, sizes), out_shape=(result...  168 us
    unnamed x2, local copies, waits for them, and re-layouts  4.13 us

profile of v1, /device:TPU:0, one launch (start us, length us, event | category | flops | bytes accessed | tf_op | source)
XLA Modules:
  0.0 174.6 jit_solution(5907303274362673788)
XLA Ops:
  0.6 0.8 slice_bitcast_fusion.1
  1.4 0.8 broadcast_subtract_fusion
  2.2 0.6 broadcast_in_dim.30.table
  2.8 167.7 %expert_layer.1 = (bf16[64,6144]{1,0:T(8,128)(2,1)}, bf16[64,6144]{1,0:T(8,128)(2,1)}) custom-call(bf16[128,6144]{1,0:T(8,128)(2,1)} %tokens.1, bf16[128,6144]{1,0:T(8,128)(2,1)} %grads.1, f32[4,8,128]{2,1,0:T(8,128)} %broadcast_in_dim.30.table, bf16[6144,1024]{1,0:T(8,128)(2,1)} %bitcast.10, bf16[6144,1024]{1,0:T(8,128)(2,1)} %bitcast.11, ...), custom_call_target="tpu_custom_call" | custom-call | flops 38654705664 | bytes 75497472 | tf_op jit(solution)/shard_map/expert_layer/pallas_call | solution.py:495
  170.5 2.1 %copy.11 = bf16[64,6144]{1,0:T(8,128)(2,1)} copy(bf16[64,6144]{1,0:T(8,128)(2,1)} %get-tuple-element.8) | data formatting | bytes 1572864
  172.5 2.1 %copy.12 = bf16[64,6144]{1,0:T(8,128)(2,1)} copy(bf16[64,6144]{1,0:T(8,128)(2,1)} %get-tuple-element.9) | data formatting | bytes 1572864
  (1 shorter events, 0.0 us)

commit v2 on v1

--- a/solution.py
+++ b/solution.py
@@ -46,6 +46,7 @@
     share_cols,
     pair_buf,
     plane_buf,
+    via_buf,
     axis_buf,
     final_buf,
     w_sem,
@@ -62,6 +63,8 @@
     r1_recv,
     r2_send,
     r2_recv,
+    via_send,
+    via_recv,
     r3_send,
     r3_recv,
     r4_send,
@@ -76,6 +79,7 @@
     total = experts * count
     rows = count // tensor
     cols = width // lanes
+    half = cols // 2
     tile_f = min(TILE, inner)
     bufs = (x_buf, g_buf)
 
@@ -90,6 +94,9 @@
 
     def col_ds(which):
         return pl.ds(pl.multiple_of(which * cols, cols), cols)
+
+    def half_ds(which, part):
+        return pl.ds(pl.multiple_of(which * cols + part * half, half), half)
 
     def remote(src, dst, send, recv, axis, target):
         return pltpu.make_async_remote_copy(
@@ -156,15 +163,21 @@
         return copies
 
     def step_two(a, k):
-        copies = []
         place = bufs[a].at[zz(experts - k), row_ds(t), col_ds(i)]
-        for m in range(1, lanes):
-            copies.append(
-                remote(place, place, d2_send.at[a, k, m], d2_recv.at[a, k, m], "dp", flip(i, m))
-            )
-        for copy in copies:
+        for m in (1, 2):
+            copy = remote(
+                place, place, d2_send.at[a, k, m], d2_recv.at[a, k, m], "dp", flip(i, m)
+            )
             copy.start()
-        return copies
+            second[a, k, m] = [copy]
+
+    def step_across(a, k, m):
+        place = bufs[a].at[zz(experts - k), row_ds(t), half_ds(flip(i, m), m - 1)]
+        copy = remote(
+            place, place, d2_send.at[a, k, m + 2], d2_recv.at[a, k, m + 2], "dp", flip(i, 3 - m)
+        )
+        copy.start()
+        second.setdefault((a, k, 3), []).append(copy)
 
     def step_three(a, k, m):
         copies = []
@@ -205,16 +218,17 @@
     second = {}
     third = {}
 
-    def relay_one(a):
-        for k in range(1, experts):
-            first[a][k - 1].wait_recv()
-            second[a, k] = step_two(a, k)
-            third[a, k, 0] = step_three(a, k, 0)
-
-    def relay_two(a, m):
-        for k in range(1, experts):
-            second[a, k][m - 1].wait_recv()
-            third[a, k, m] = step_three(a, k, m)
+    def relay_one(a, k):
+        first[a][k - 1].wait_recv()
+        step_two(a, k)
+        third[a, k, 0] = step_three(a, k, 0)
+
+    def relay_two(a, k, m):
+        for copy in second[a, k, m]:
+            copy.wait_recv()
+        if m < 3:
+            step_across(a, k, m)
+        third[a, k, m] = step_three(a, k, m)
 
     def arrived(a, m):
         for k in range(1, experts):
@@ -225,8 +239,9 @@
         for copy in first[a]:
             copy.wait_send()
         for k in range(1, experts):
-            for copy in second[a, k]:
-                copy.wait_send()
+            for m in range(1, lanes):
+                for copy in second[a, k, m]:
+                    copy.wait_send()
             for m in range(lanes):
                 for copy in third[a, k, m]:
                     copy.wait_send()
@@ -234,14 +249,18 @@
     def operand(a, m):
         return bufs[a][:, :, col_ds(flip(i, m))].reshape(total, cols)
 
-    relay_one(0)
+    others = list(range(1, experts))
+    for k in others:
+        relay_one(0, k)
     first[1] = step_one(1)
     own[0].wait()
     for m in range(lanes):
         if m + 1 < lanes:
-            relay_two(0, m + 1)
-        else:
-            relay_one(1)
+            for k in others:
+                relay_two(0, k, m + 1)
+        for k in others:
+            if m == min(k, lanes - 1):
+                relay_one(1, k)
         arrived(0, m)
         slot = m % 2
         fetched(0, slot)
@@ -289,6 +308,8 @@
 
     pairs = {}
     planes = {}
+    vias = {}
+    order = others + [0]
 
     def pair_send(a, m):
         copies = []
@@ -320,19 +341,44 @@
             return carry
 
         lax.fori_loop(0, experts, add, 0)
-        if m == 0:
-            return
-        for k in list(range(1, experts)) + [0]:
-            copy = remote(
-                bufs[a].at[zz(k), row_ds(t), block],
-                plane_buf.at[a, m - 1, zz(k)],
-                r2_send.at[a, m, k],
-                r2_recv.at[a, m, k],
-                "dp",
-                flip(i, m),
-            )
-            copy.start()
-            planes[a, m, k] = copy
+        for k in order:
+            if m == 3:
+                for part in range(2):
+                    copy = remote(
+                        bufs[a].at[zz(k), row_ds(t), half_ds(flip(i, 3), part)],
+                        via_buf.at[a, part, zz(k)],
+                        via_send.at[a, part, k],
+                        via_recv.at[a, part, k],
+                        "dp",
+                        flip(i, part + 1),
+                    )
+                    copy.start()
+                    vias[a, part, k] = copy
+            elif m > 0:
+                plane_send(a, m, k, m - 1)
+
+    def plane_send(a, m, k, part):
+        copy = remote(
+            bufs[a].at[zz(k), row_ds(t), half_ds(flip(i, m), part)],
+            plane_buf.at[a, m - 1, zz(k), :, part * half : (part + 1) * half],
+            r2_send.at[a, m - 1, part, k],
+            r2_recv.at[a, m - 1, part, k],
+            "dp",
+            flip(i, m),
+        )
+        copy.start()
+        planes[a, m, part, k] = copy
+
+    def via_sum(a):
+        for k in order:
+            for part in range(2):
+                m = 2 - part
+                vias[a, part, k].wait_recv()
+                place = bufs[a].at[zz(k), row_ds(t), half_ds(flip(i, m), part)]
+                value = place[...].astype(jnp.float32)
+                value = value + via_buf[a, part, zz(k)].astype(jnp.float32)
+                place[...] = value.astype(jnp.bfloat16)
+                plane_send(a, m, k, part)
 
     for n in range(lanes):
         m = lanes - 1 - n
@@ -352,13 +398,17 @@
         pair_send(0, m)
         if n > 0:
             pair_sum(0, m + 1)
-    relay_two(1, 1)
+            for k in others:
+                if n == min(k, lanes - 1):
+                    relay_two(1, k, 1)
+                    relay_two(1, k, 2)
     pair_sum(0, 0)
 
     own[1].wait()
     for m in range(lanes):
-        if 1 <= m < lanes - 1:
-            relay_two(1, m + 1)
+        if m == lanes - 2:
+            for k in others:
+                relay_two(1, k, 3)
         arrived(1, m)
         slot = (lanes - 1 - m) % 2
         fetched(2, slot)
@@ -421,18 +471,23 @@
             fetch(0, m - 2, slot)
             fetch(1, m - 2, slot)
         pair_send(1, m)
-        if n > 0:
+        if n == 0:
+            via_sum(0)
+        else:
             pair_sum(1, m + 1)
     pair_sum(1, 0)
 
     crossing = {}
     for a in range(2):
-        for k in list(range(1, experts)) + [0]:
-            for m in range(1, lanes):
-                planes[a, m, k].wait_recv()
+        if a == 1:
+            via_sum(1)
+        for k in order:
+            for m in (1, 2):
+                for part in range(2):
+                    planes[a, m, part, k].wait_recv()
             place = bufs[a].at[zz(k), row_ds(t), col_ds(i)]
             value = place[...].astype(jnp.float32)
-            for m in range(1, lanes):
+            for m in (1, 2):
                 value = value + plane_buf[a, m - 1, zz(k)].astype(jnp.float32)
             place[...] = value.astype(jnp.bfloat16)
             if k > 0:
@@ -466,6 +521,8 @@
     for copies in pairs.values():
         for copy in copies:
             copy.wait_send()
+    for copy in vias.values():
+        copy.wait_send()
     for copy in planes.values():
         copy.wait_send()
     for copy in crossing.values():
@@ -511,7 +568,8 @@
             pltpu.VMEM((experts, 8, count), f32),
             pltpu.VMEM((total, count), f32),
             pltpu.VMEM((2, lanes, tensor - 1, experts, rows, cols), bf16),
-            pltpu.VMEM((2, lanes - 1, experts, rows, cols), bf16),
+            pltpu.VMEM((2, 2, experts, rows, cols), bf16),
+            pltpu.VMEM((2, 2, experts, rows, cols // 2), bf16),
             pltpu.VMEM((2, experts - 1, rows, cols), bf16),
             pltpu.VMEM((2, rows, cols), bf16),
             dma((3, 2)),
@@ -520,14 +578,16 @@
             dma((experts,)),
             dma((2, experts)),
             dma((2, experts)),
-            dma((2, experts, lanes)),
-            dma((2, experts, lanes)),
+            dma((2, experts, 5)),
+            dma((2, experts, 5)),
             dma((2, experts, lanes, tensor)),
             dma((2, experts, lanes, tensor)),
             dma((2, lanes, tensor)),
             dma((2, lanes, tensor)),
-            dma((2, lanes, experts)),
-            dma((2, lanes, experts)),
+            dma((2, 2, 2, experts)),
+            dma((2, 2, 2, experts)),
+            dma((2, 2, experts)),
+            dma((2, 2, experts)),
             dma((2, experts)),
             dma((2, experts)),
             dma((2, lanes)),

time: 176 us -> 164 us (0.932)
  Pallas kernels: 168 us -> 154 us
    pallas_call x1, Pallas kernels: 168 us -> 154 us  [local(): pl.pallas_call(functools.partial(expert_kernel, sizes), out_shape=(result...]
where the time goes in v2:
time: 164 us; the launch traced here: 161 us
  Pallas kernels  154 us (94%)
  local copies, waits for them, and re-layouts  5.5 us (3%)
    pallas_call x1, Pallas kernels, local(): pl.pallas_call(functools.partial(expert_kernel, sizes), out_shape=(result...  154 us
    unnamed x2, local copies, waits for them, and re-layouts  4.13 us

profile of v2, /device:TPU:0, one launch (start us, length us, event | category | flops | bytes accessed | tf_op | source)
XLA Modules:
  0.0 161.3 jit_solution(16754982383428098739)
XLA Ops:
  0.6 0.8 slice_bitcast_fusion.1
  1.4 0.8 broadcast_subtract_fusion
  2.2 0.6 broadcast_in_dim.30.table
  2.8 154.4 %expert_layer.1 = (bf16[64,6144]{1,0:T(8,128)(2,1)}, bf16[64,6144]{1,0:T(8,128)(2,1)}) custom-call(bf16[128,6144]{1,0:T(8,128)(2,1)} %tokens.1, bf16[128,6144]{1,0:T(8,128)(2,1)} %grads.1, f32[4,8,128]{2,1,0:T(8,128)} %broadcast_in_dim.30.table, bf16[6144,1024]{1,0:T(8,128)(2,1)} %bitcast.10, bf16[6144,1024]{1,0:T(8,128)(2,1)} %bitcast.11, ...), custom_call_target="tpu_custom_call" | custom-call | flops 38654705664 | bytes 75497472 | tf_op jit(solution)/shard_map/expert_layer/pallas_call | solution.py:552
  157.2 2.1 %copy.11 = bf16[64,6144]{1,0:T(8,128)(2,1)} copy(bf16[64,6144]{1,0:T(8,128)(2,1)} %get-tuple-element.8) | data formatting | bytes 1572864
  159.2 2.1 %copy.12 = bf16[64,6144]{1,0:T(8,128)(2,1)} copy(bf16[64,6144]{1,0:T(8,128)(2,1)} %get-tuple-element.9) | data formatting | bytes 1572864
  (1 shorter events, 0.0 us)

commit v3 on v2

--- a/solution.py
+++ b/solution.py
@@ -9,7 +9,8 @@
 
 MESH = pl.DeviceIdType.MESH
 CONTRACT_LAST = (((1,), (1,)), ((), ()))
-TILE = 256
+TILE = 512
+GROUPS = (1, 2)
 
 
 def flip(index, mask):
@@ -108,26 +109,27 @@
             device_id_type=MESH,
         )
 
-    def load(kind, m, slot):
-        block = col_ds(flip(i, m))
-        if kind == 0:
-            pair = (w_gate.at[block, :], wg_buf.at[slot])
-        elif kind == 1:
-            pair = (w_up.at[block, :], wu_buf.at[slot])
-        else:
-            pair = (w_down.at[:, block], wd_buf.at[slot])
-        return pltpu.make_async_copy(*pair, w_sem.at[kind, slot])
-
     loads = {}
 
-    def fetch(kind, m, slot):
-        loads[kind, slot] = load(kind, m, slot)
-        loads[kind, slot].start()
-
-    def fetched(kind, slot):
-        copy = loads.pop((kind, slot), None)
-        if copy is not None:
-            copy.wait()
+    def fetch(kind, m, slot, parts=(0, 1)):
+        for part in parts:
+            source = half_ds(flip(i, m), part)
+            to = pl.ds(part * half, half)
+            if kind == 0:
+                pair = (w_gate.at[source, :], wg_buf.at[slot, to, :])
+            elif kind == 1:
+                pair = (w_up.at[source, :], wu_buf.at[slot, to, :])
+            else:
+                pair = (w_down.at[:, source], wd_buf.at[slot, :, to])
+            copy = pltpu.make_async_copy(*pair, w_sem.at[kind, slot, part])
+            copy.start()
+            loads[kind, slot, part] = copy
+
+    def fetched(kind, slot, parts=(0, 1)):
+        for part in parts:
+            copy = loads.pop((kind, slot, part), None)
+            if copy is not None:
+                copy.wait()
 
     own = [
         pltpu.make_async_copy(tokens, x_buf.at[z], own_sem.at[0]),
@@ -311,32 +313,50 @@
     vias = {}
     order = others + [0]
 
-    def pair_send(a, m):
+    def group_size(a):
+        return cols // GROUPS[a]
+
+    def group_ds(a, g, m):
+        size = group_size(a)
+        return pl.ds(pl.multiple_of(flip(i, m) * cols + g * size, size), size)
+
+    def part_ds(a, g, m, part):
+        size = group_size(a) // 2
+        start = flip(i, m) * cols + (2 * g + part) * size
+        return pl.ds(pl.multiple_of(start, size), size)
+
+    def inside(a, g, part=None):
+        size = group_size(a)
+        if part is None:
+            return pl.ds(g * size, size)
+        return pl.ds((2 * g + part) * (size // 2), size // 2)
+
+    def pair_send(a, g, m):
         copies = []
         for s in range(1, tensor):
             copies.append(
                 remote(
-                    bufs[a].at[:, row_ds(tt(s)), col_ds(flip(i, m))],
-                    pair_buf.at[a, m, s - 1],
-                    r1_send.at[a, m, s],
-                    r1_recv.at[a, m, s],
+                    bufs[a].at[:, row_ds(tt(s)), group_ds(a, g, m)],
+                    pair_buf.at[a, m, s - 1, :, :, inside(a, g)],
+                    r1_send.at[a, g, m, s],
+                    r1_recv.at[a, g, m, s],
                     "tensor",
                     tt(s),
                 )
             )
         for copy in copies:
             copy.start()
-        pairs[a, m] = copies
-
-    def pair_sum(a, m):
-        for copy in pairs[a, m]:
+        pairs[a, g, m] = copies
+
+    def pair_sum(a, g, m):
+        for copy in pairs[a, g, m]:
             copy.wait_recv()
-        block = col_ds(flip(i, m))
+        block = group_ds(a, g, m)
 
         def add(e, carry):
             value = bufs[a][e, row_ds(t), block].astype(jnp.float32)
             for s in range(tensor - 1):
-                value = value + pair_buf[a, m, s, e].astype(jnp.float32)
+                value = value + pair_buf[a, m, s, e, :, inside(a, g)].astype(jnp.float32)
             bufs[a][e, row_ds(t), block] = value.astype(jnp.bfloat16)
             return carry
 
@@ -345,40 +365,89 @@
             if m == 3:
                 for part in range(2):
                     copy = remote(
-                        bufs[a].at[zz(k), row_ds(t), half_ds(flip(i, 3), part)],
-                        via_buf.at[a, part, zz(k)],
-                        via_send.at[a, part, k],
-                        via_recv.at[a, part, k],
+                        bufs[a].at[zz(k), row_ds(t), part_ds(a, g, 3, part)],
+                        via_buf.at[a, part, zz(k), :, inside_via(a, g)],
+                        via_send.at[a, g, part, k],
+                        via_recv.at[a, g, part, k],
                         "dp",
                         flip(i, part + 1),
                     )
                     copy.start()
-                    vias[a, part, k] = copy
+                    vias[a, g, part, k] = copy
             elif m > 0:
-                plane_send(a, m, k, m - 1)
-
-    def plane_send(a, m, k, part):
+                plane_send(a, g, m, k, m - 1)
+
+    def inside_via(a, g):
+        size = group_size(a) // 2
+        return pl.ds(g * size, size)
+
+    def plane_send(a, g, m, k, part):
         copy = remote(
-            bufs[a].at[zz(k), row_ds(t), half_ds(flip(i, m), part)],
-            plane_buf.at[a, m - 1, zz(k), :, part * half : (part + 1) * half],
-            r2_send.at[a, m - 1, part, k],
-            r2_recv.at[a, m - 1, part, k],
+            bufs[a].at[zz(k), row_ds(t), part_ds(a, g, m, part)],
+            plane_buf.at[a, m - 1, zz(k), :, inside(a, g, part)],
+            r2_send.at[a, g, m - 1, part, k],
+            r2_recv.at[a, g, m - 1, part, k],
             "dp",
             flip(i, m),
         )
         copy.start()
-        planes[a, m, part, k] = copy
-
-    def via_sum(a):
+        planes[a, g, m, part, k] = copy
+
+    def via_sum(a, g):
         for k in order:
             for part in range(2):
                 m = 2 - part
-                vias[a, part, k].wait_recv()
-                place = bufs[a].at[zz(k), row_ds(t), half_ds(flip(i, m), part)]
+                vias[a, g, part, k].wait_recv()
+                place = bufs[a].at[zz(k), row_ds(t), part_ds(a, g, m, part)]
                 value = place[...].astype(jnp.float32)
-                value = value + via_buf[a, part, zz(k)].astype(jnp.float32)
+                value = value + via_buf[a, part, zz(k), :, inside_via(a, g)].astype(jnp.float32)
                 place[...] = value.astype(jnp.bfloat16)
-                plane_send(a, m, k, part)
+                plane_send(a, g, m, k, part)
+
+    crossing = {}
+    finals = []
+
+    def plane_sum(a, g):
+        for k in order:
+            for m in (1, 2):
+                for part in range(2):
+                    planes[a, g, m, part, k].wait_recv()
+            place = bufs[a].at[zz(k), row_ds(t), group_ds(a, g, 0)]
+            value = place[...].astype(jnp.float32)
+            for m in (1, 2):
+                value = value + plane_buf[a, m - 1, zz(k), :, inside(a, g)].astype(jnp.float32)
+            place[...] = value.astype(jnp.bfloat16)
+            if k > 0:
+                copy = remote(
+                    place,
+                    axis_buf.at[a, k - 1, :, inside(a, g)],
+                    r3_send.at[a, g, k],
+                    r3_recv.at[a, g, k],
+                    "expert",
+                    zz(k),
+                )
+                copy.start()
+                crossing[a, g, k] = copy
+
+    def finish(a, g):
+        value = bufs[a][z, row_ds(t), group_ds(a, g, 0)].astype(jnp.float32)
+        for k in others:
+            crossing[a, g, k].wait_recv()
+            value = value + axis_buf[a, k - 1, :, inside(a, g)].astype(jnp.float32)
+        source = final_buf.at[a, :, inside(a, g)]
+        source[...] = value.astype(jnp.bfloat16)
+        target = (out_hbm, back_hbm)[a].at[:, group_ds(a, g, 0)]
+        copies = []
+        for m in range(lanes - 1, 0, -1):
+            copies.append(
+                remote(
+                    source, target, r4_send.at[a, g, m], r4_recv.at[a, g, m], "dp", flip(i, m)
+                )
+            )
+        copies.append(pltpu.make_async_copy(source, target, own_sem.at[3 + 2 * a + g]))
+        for copy in copies:
+            copy.start()
+        finals.extend(copies)
 
     for n in range(lanes):
         m = lanes - 1 - n
@@ -386,23 +455,23 @@
         fetched(2, slot)
 
         def down(c, carry, m=m, slot=slot):
-            span = pl.ds(pl.multiple_of(c * TILE, TILE), TILE)
-            to = pl.ds(pl.multiple_of(flip(i, m) * cols + c * TILE, TILE), TILE)
+            span = pl.ds(pl.multiple_of(c * half, half), half)
+            to = half_ds(flip(i, m), c)
             value = jnp.dot(hid[...], wd_buf[slot, :, span], preferred_element_type=jnp.float32)
-            x_buf[:, :, to] = value.astype(jnp.bfloat16).reshape(experts, count, TILE)
+            x_buf[:, :, to] = value.astype(jnp.bfloat16).reshape(experts, count, half)
             return carry
 
-        lax.fori_loop(0, cols // TILE, down, 0)
+        lax.fori_loop(0, 2, down, 0)
         if n + 2 < lanes:
             fetch(2, lanes - 1 - (n + 2), slot)
-        pair_send(0, m)
+        pair_send(0, 0, m)
         if n > 0:
-            pair_sum(0, m + 1)
+            pair_sum(0, 0, m + 1)
             for k in others:
                 if n == min(k, lanes - 1):
                     relay_two(1, k, 1)
                     relay_two(1, k, 2)
-    pair_sum(0, 0)
+    pair_sum(0, 0, 0)
 
     own[1].wait()
     for m in range(lanes):
@@ -448,76 +517,40 @@
     lax.fori_loop(0, experts, differentiate, 0)
     sent(1)
 
-    for n in range(lanes):
-        m = lanes - 1 - n
+    steps = [(g, m) for g in range(2) for m in range(lanes - 1, -1, -1)]
+    for step, (g, m) in enumerate(steps):
         slot = m % 2
-        fetched(0, slot)
-        fetched(1, slot)
-
-        def back(c, carry, m=m, slot=slot):
-            span = pl.ds(pl.multiple_of(c * TILE, TILE), TILE)
-            to = pl.ds(pl.multiple_of(flip(i, m) * cols + c * TILE, TILE), TILE)
-            value = lax.dot_general(
-                hid[...], wg_buf[slot, span, :], CONTRACT_LAST, preferred_element_type=jnp.float32
-            )
-            value = value + lax.dot_general(
-                gu[...], wu_buf[slot, span, :], CONTRACT_LAST, preferred_element_type=jnp.float32
-            )
-            g_buf[:, :, to] = value.astype(jnp.bfloat16).reshape(experts, count, TILE)
-            return carry
-
-        lax.fori_loop(0, cols // TILE, back, 0)
-        if n + 2 < lanes:
-            fetch(0, m - 2, slot)
-            fetch(1, m - 2, slot)
-        pair_send(1, m)
-        if n == 0:
-            via_sum(0)
-        else:
-            pair_sum(1, m + 1)
-    pair_sum(1, 0)
-
-    crossing = {}
-    for a in range(2):
-        if a == 1:
-            via_sum(1)
-        for k in order:
-            for m in (1, 2):
-                for part in range(2):
-                    planes[a, m, part, k].wait_recv()
-            place = bufs[a].at[zz(k), row_ds(t), col_ds(i)]
-            value = place[...].astype(jnp.float32)
-            for m in (1, 2):
-                value = value + plane_buf[a, m - 1, zz(k)].astype(jnp.float32)
-            place[...] = value.astype(jnp.bfloat16)
-            if k > 0:
-                copy = remote(
-                    place,
-                    axis_buf.at[a, k - 1],
-                    r3_send.at[a, k],
-                    r3_recv.at[a, k],
-                    "expert",
-                    zz(k),
-                )
-                copy.start()
-                crossing[a, k] = copy
-    finals = []
-    for a in range(2):
-        value = bufs[a][z, row_ds(t), col_ds(i)].astype(jnp.float32)
-        for k in range(1, experts):
-            crossing[a, k].wait_recv()
-            value = value + axis_buf[a, k - 1].astype(jnp.float32)
-        final_buf[a] = value.astype(jnp.bfloat16)
-        target = (out_hbm, back_hbm)[a].at[:, col_ds(i)]
-        for m in range(1, lanes):
-            finals.append(
-                remote(
-                    final_buf.at[a], target, r4_send.at[a, m], r4_recv.at[a, m], "dp", flip(i, m)
-                )
-            )
-        finals.append(pltpu.make_async_copy(final_buf.at[a], target, own_sem.at[3 + a]))
-        for copy in finals[-lanes:]:
-            copy.start()
+        fetched(0, slot, (g,))
+        fetched(1, slot, (g,))
+        span = slice(g * half, (g + 1) * half)
+        value = lax.dot_general(
+            hid[...], wg_buf[slot, span, :], CONTRACT_LAST, preferred_element_type=jnp.float32
+        )
+        value = value + lax.dot_general(
+            gu[...], wu_buf[slot, span, :], CONTRACT_LAST, preferred_element_type=jnp.float32
+        )
+        g_buf[:, :, half_ds(flip(i, m), g)] = value.astype(jnp.bfloat16).reshape(
+            experts, count, half
+        )
+        if m >= 2:
+            fetch(0, m - 2, slot, (g,))
+            fetch(1, m - 2, slot, (g,))
+        pair_send(1, g, m)
+        if step > 0:
+            pair_sum(1, *steps[step - 1])
+        if step == 0:
+            via_sum(0, 0)
+        if step == 4:
+            plane_sum(0, 0)
+        if step == 5:
+            via_sum(1, 0)
+    pair_sum(1, 1, 0)
+    finish(0, 0)
+    plane_sum(1, 0)
+    via_sum(1, 1)
+    finish(1, 0)
+    plane_sum(1, 1)
+    finish(1, 1)
     for copies in pairs.values():
         for copy in copies:
             copy.wait_send()
@@ -572,8 +605,8 @@
             pltpu.VMEM((2, 2, experts, rows, cols // 2), bf16),
             pltpu.VMEM((2, experts - 1, rows, cols), bf16),
             pltpu.VMEM((2, rows, cols), bf16),
-            dma((3, 2)),
-            dma((5,)),
+            dma((3, 2, 2)),
+            dma((7,)),
             dma((experts,)),
             dma((experts,)),
             dma((2, experts)),
@@ -582,16 +615,16 @@
             dma((2, experts, 5)),
             dma((2, experts, lanes, tensor)),
             dma((2, experts, lanes, tensor)),
-            dma((2, lanes, tensor)),
-            dma((2, lanes, tensor)),
+            dma((2, 2, lanes, tensor)),
+            dma((2, 2, lanes, tensor)),
+            dma((2, 2, 2, 2, experts)),
+            dma((2, 2, 2, 2, experts)),
             dma((2, 2, 2, experts)),
             dma((2, 2, 2, experts)),
             dma((2, 2, experts)),
             dma((2, 2, experts)),
-            dma((2, experts)),
-            dma((2, experts)),
-            dma((2, lanes)),
-            dma((2, lanes)),
+            dma((2, 2, lanes)),
+            dma((2, 2, lanes)),
         ],
         compiler_params=pltpu.CompilerParams(
             collective_id=0, has_side_effects=True, vmem_limit_bytes=62 * 1024 * 1024

time: 164 us -> 155 us (0.945); the launches traced: 161 us -> 155 us
  Pallas kernels: 154 us -> 148 us
    pallas_call x1, Pallas kernels: 154 us -> 148 us  [local(): pl.pallas_call(functools.partial(expert_kernel, sizes), out_shape=(result...]
where the time goes in v3:
time: 155 us
  Pallas kernels  148 us (95%)
  local copies, waits for them, and re-layouts  5.5 us (4%)
    pallas_call x1, Pallas kernels, local(): pl.pallas_call(functools.partial(expert_kernel, sizes), out_shape=(result...  148 us
    unnamed x2, local copies, waits for them, and re-layouts  4.13 us

profile of v3, /device:TPU:0, one launch (start us, length us, event | category | flops | bytes accessed | tf_op | source)
XLA Modules:
  0.0 155.0 jit_solution(5626580219941321692)
XLA Ops:
  0.6 0.8 slice_bitcast_fusion.1
  1.4 0.8 broadcast_subtract_fusion
  2.2 0.6 broadcast_in_dim.30.table
  2.8 148.1 %expert_layer.1 = (bf16[64,6144]{1,0:T(8,128)(2,1)}, bf16[64,6144]{1,0:T(8,128)(2,1)}) custom-call(bf16[128,6144]{1,0:T(8,128)(2,1)} %tokens.1, bf16[128,6144]{1,0:T(8,128)(2,1)} %grads.1, f32[4,8,128]{2,1,0:T(8,128)} %broadcast_in_dim.30.table, bf16[6144,1024]{1,0:T(8,128)(2,1)} %bitcast.10, bf16[6144,1024]{1,0:T(8,128)(2,1)} %bitcast.11, ...), custom_call_target="tpu_custom_call" | custom-call | flops 38654705664 | bytes 75497472 | tf_op jit(solution)/shard_map/expert_layer/pallas_call | solution.py:585
  150.9 2.1 %copy.11 = bf16[64,6144]{1,0:T(8,128)(2,1)} copy(bf16[64,6144]{1,0:T(8,128)(2,1)} %get-tuple-element.8) | data formatting | bytes 1572864
  153.0 2.1 %copy.12 = bf16[64,6144]{1,0:T(8,128)(2,1)} copy(bf16[64,6144]{1,0:T(8,128)(2,1)} %get-tuple-element.9) | data formatting | bytes 1572864
  (1 shorter events, 0.0 us)

commit v4 on v3

--- a/solution.py
+++ b/solution.py
@@ -146,23 +146,20 @@
         pl.semaphore_signal(barrier, inc=1, device_id={"tensor": tt(s)}, device_id_type=MESH)
     pl.semaphore_wait(barrier, experts + lanes + tensor - 3)
 
-    def step_one(a):
-        copies = []
-        source = (tokens, grads)[a]
-        for k in range(1, experts):
-            copies.append(
-                remote(
-                    source.at[row_ds(t), col_ds(i)],
-                    bufs[a].at[z, row_ds(t), col_ds(i)],
-                    d1_send.at[a, k],
-                    d1_recv.at[a, k],
-                    "expert",
-                    zz(k),
-                )
-            )
-        for copy in copies:
-            copy.start()
-        return copies
+    others = sorted(range(1, experts), key=lambda k: min(k, experts - k))
+    first = {}
+
+    def step_one(a, k):
+        copy = remote(
+            (tokens, grads)[a].at[row_ds(t), col_ds(i)],
+            bufs[a].at[z, row_ds(t), col_ds(i)],
+            d1_send.at[a, k],
+            d1_recv.at[a, k],
+            "expert",
+            zz(k),
+        )
+        copy.start()
+        first[a, k] = copy
 
     def step_two(a, k):
         place = bufs[a].at[zz(experts - k), row_ds(t), col_ds(i)]
@@ -194,7 +191,7 @@
             copy.start()
         return copies
 
-    first = {0: step_one(0)}
+    step_one(0, others[0])
     shares = []
     for k in range(1, experts):
         shares.append(
@@ -219,9 +216,10 @@
 
     second = {}
     third = {}
+    left = set()
 
     def relay_one(a, k):
-        first[a][k - 1].wait_recv()
+        first[a, k].wait_recv()
         step_two(a, k)
         third[a, k, 0] = step_three(a, k, 0)
 
@@ -238,9 +236,9 @@
                 copy.wait_recv()
 
     def sent(a):
-        for copy in first[a]:
-            copy.wait_send()
-        for k in range(1, experts):
+        for k in others:
+            if (a, k) not in left:
+                first[a, k].wait_send()
             for m in range(1, lanes):
                 for copy in second[a, k, m]:
                     copy.wait_send()
@@ -251,18 +249,33 @@
     def operand(a, m):
         return bufs[a][:, :, col_ds(flip(i, m))].reshape(total, cols)
 
-    others = list(range(1, experts))
-    for k in others:
+    def follow(a, k, b, n):
+        first[a, k].wait_send()
+        left.add((a, k))
+        step_one(b, n)
+
+    for n, k in enumerate(others):
+        if n + 1 < len(others):
+            follow(0, k, 0, others[n + 1])
+        else:
+            follow(0, k, 1, others[0])
         relay_one(0, k)
-    first[1] = step_one(1)
+        if n > 0:
+            relay_two(0, others[n - 1], 1)
+            relay_two(0, others[n - 1], 2)
     own[0].wait()
     for m in range(lanes):
-        if m + 1 < lanes:
+        if m == 1:
+            relay_two(0, others[-1], 1)
+            relay_two(0, others[-1], 2)
+        for n, k in enumerate(others):
+            if m == min(n + 1, lanes - 1):
+                if n + 1 < len(others):
+                    follow(1, k, 1, others[n + 1])
+                relay_one(1, k)
+        if m == lanes - 1:
             for k in others:
-                relay_two(0, k, m + 1)
-        for k in others:
-            if m == min(k, lanes - 1):
-                relay_one(1, k)
+                relay_two(0, k, 3)
         arrived(0, m)
         slot = m % 2
         fetched(0, slot)
@@ -311,7 +324,7 @@
     pairs = {}
     planes = {}
     vias = {}
-    order = others + [0]
+    order = others[::-1] + [0]
 
     def group_size(a):
         return cols // GROUPS[a]
@@ -467,8 +480,8 @@
         pair_send(0, 0, m)
         if n > 0:
             pair_sum(0, 0, m + 1)
-            for k in others:
-                if n == min(k, lanes - 1):
+            for j, k in enumerate(others):
+                if n == min(j + 1, lanes - 1):
                     relay_two(1, k, 1)
                     relay_two(1, k, 2)
     pair_sum(0, 0, 0)
@@ -564,6 +577,21 @@
         copy.wait()
 
 
+def hand_over(out, back, out_copy, back_copy, sem):
+    rows = out.shape[0]
+    parts = 4 if rows % 64 == 0 else 1
+    span = rows // parts
+    copies = []
+    for a, (source, target) in enumerate(((out, out_copy), (back, back_copy))):
+        for n in range(parts):
+            part = pl.ds(n * span, span)
+            copies.append(pltpu.make_async_copy(source.at[part], target.at[part], sem.at[a, n]))
+    for copy in copies:
+        copy.start()
+    for copy in copies:
+        copy.wait()
+
+
 def local(sizes, tokens, routes, logits, grad_out, w_gate, w_up, w_down):
     lanes, experts, tensor = sizes
     count, width = tokens.shape
@@ -582,7 +610,7 @@
     result = jax.ShapeDtypeStruct((rows, width), bf16)
     anywhere = pl.BlockSpec(memory_space=pl.ANY)
     flops = 2 * total * width * inner * 6
-    return pl.pallas_call(
+    results = pl.pallas_call(
         functools.partial(expert_kernel, sizes),
         out_shape=(result, result),
         in_specs=[anywhere] * 6,
@@ -634,6 +662,14 @@
         ),
         name="expert_layer",
     )(tokens, grad_out, table, w_gate[0], w_up[0], w_down[0])
+    return pl.pallas_call(
+        hand_over,
+        out_shape=(result, result),
+        in_specs=[anywhere] * 2,
+        out_specs=(anywhere, anywhere),
+        scratch_shapes=[dma((2, 4))],
+        name="hand_over",
+    )(*results)
 
 
 def solution(mesh):

time: 155 us -> 205 us (1.32)
  Pallas kernels: 148 us -> 201 us
  local copies, waits for them, and re-layouts: 5.5 us -> 1.38 us
    pallas_call x0 -> x1, Pallas kernels: none -> 48.8 us  [local(): pl.pallas_call(hand_over, out_shape=(result, result), in_specs=[anywhere]...]
    pallas_call x1, Pallas kernels: 148 us -> 153 us  [local(): pl.pallas_call(functools.partial(expert_kernel, sizes), out_shape=(result...]
    unnamed x2 -> x0, local copies, waits for them, and re-layouts: 4.13 us -> none
where the time goes in v4:
time: 205 us; the launch traced here: 204 us
  Pallas kernels  201 us (98%)
    pallas_call x1, Pallas kernels, local(): pl.pallas_call(functools.partial(expert_kernel, sizes), out_shape=(result...  153 us
    pallas_call x1, Pallas kernels, local(): pl.pallas_call(hand_over, out_shape=(result, result), in_specs=[anywhere]...  48.8 us

profile of v4, /device:TPU:0, one launch (start us, length us, event | category | flops | bytes accessed | tf_op | source)
XLA Modules:
  0.0 204.3 jit_solution(4016873066995251448)
XLA Ops:
  0.6 0.8 slice_bitcast_fusion.1
  1.4 0.8 broadcast_subtract_fusion
  2.2 0.6 broadcast_in_dim.30.table
  2.8 152.6 %expert_layer.1 = (bf16[64,6144]{1,0:T(8,128)(2,1)}, bf16[64,6144]{1,0:T(8,128)(2,1)}) custom-call(bf16[128,6144]{1,0:T(8,128)(2,1)} %tokens.1, bf16[128,6144]{1,0:T(8,128)(2,1)} %grads.1, f32[4,8,128]{2,1,0:T(8,128)} %broadcast_in_dim.30.table, bf16[6144,1024]{1,0:T(8,128)(2,1)} %bitcast.10, bf16[6144,1024]{1,0:T(8,128)(2,1)} %bitcast.11, ...), custom_call_target="tpu_custom_call" | custom-call | flops 38654705664 | bytes 75497472 | tf_op jit(solution)/shard_map/expert_layer/pallas_call | solution.py:613
  155.3 48.8 %hand_over.1 = (bf16[64,6144]{1,0:T(8,128)(2,1)}, bf16[64,6144]{1,0:T(8,128)(2,1)}) custom-call(bf16[64,6144]{1,0:T(8,128)(2,1)} %get-tuple-element.4.out, bf16[64,6144]{1,0:T(8,128)(2,1)} %get-tuple-element.5.back), custom_call_target="tpu_custom_call" | custom-call | tf_op jit(solution)/shard_map/hand_over/pallas_call | solution.py:665
  (1 shorter events, 0.0 us)

commit v5 on v3

--- a/solution.py
+++ b/solution.py
@@ -10,7 +10,7 @@
 MESH = pl.DeviceIdType.MESH
 CONTRACT_LAST = (((1,), (1,)), ((), ()))
 TILE = 512
-GROUPS = (1, 2)
+GROUPS = (1, 3)
 
 
 def flip(index, mask):
@@ -81,6 +81,7 @@
     rows = count // tensor
     cols = width // lanes
     half = cols // 2
+    slim = cols // 3
     tile_f = min(TILE, inner)
     bufs = (x_buf, g_buf)
 
@@ -98,6 +99,9 @@
 
     def half_ds(which, part):
         return pl.ds(pl.multiple_of(which * cols + part * half, half), half)
+
+    def slim_ds(which, part):
+        return pl.ds(pl.multiple_of(which * cols + part * slim, slim), slim)
 
     def remote(src, dst, send, recv, axis, target):
         return pltpu.make_async_remote_copy(
@@ -111,10 +115,10 @@
 
     loads = {}
 
-    def fetch(kind, m, slot, parts=(0, 1)):
+    def fetch(kind, m, slot, parts=(0, 1, 2)):
         for part in parts:
-            source = half_ds(flip(i, m), part)
-            to = pl.ds(part * half, half)
+            source = slim_ds(flip(i, m), part)
+            to = pl.ds(part * slim, slim)
             if kind == 0:
                 pair = (w_gate.at[source, :], wg_buf.at[slot, to, :])
             elif kind == 1:
@@ -125,7 +129,7 @@
             copy.start()
             loads[kind, slot, part] = copy
 
-    def fetched(kind, slot, parts=(0, 1)):
+    def fetched(kind, slot, parts=(0, 1, 2)):
         for part in parts:
             copy = loads.pop((kind, slot, part), None)
             if copy is not None:
@@ -444,7 +448,7 @@
                     source, target, r4_send.at[a, g, m], r4_recv.at[a, g, m], "dp", flip(i, m)
                 )
             )
-        copies.append(pltpu.make_async_copy(source, target, own_sem.at[3 + 2 * a + g]))
+        copies.append(pltpu.make_async_copy(source, target, own_sem.at[3 + 3 * a + g]))
         for copy in copies:
             copy.start()
         finals.extend(copies)
@@ -517,20 +521,20 @@
     lax.fori_loop(0, experts, differentiate, 0)
     sent(1)
 
-    steps = [(g, m) for g in range(2) for m in range(lanes - 1, -1, -1)]
+    steps = [(g, m) for g in range(3) for m in range(lanes - 1, -1, -1)]
     for step, (g, m) in enumerate(steps):
         slot = m % 2
         fetched(0, slot, (g,))
         fetched(1, slot, (g,))
-        span = slice(g * half, (g + 1) * half)
+        span = slice(g * slim, (g + 1) * slim)
         value = lax.dot_general(
             hid[...], wg_buf[slot, span, :], CONTRACT_LAST, preferred_element_type=jnp.float32
         )
         value = value + lax.dot_general(
             gu[...], wu_buf[slot, span, :], CONTRACT_LAST, preferred_element_type=jnp.float32
         )
-        g_buf[:, :, half_ds(flip(i, m), g)] = value.astype(jnp.bfloat16).reshape(
-            experts, count, half
+        g_buf[:, :, slim_ds(flip(i, m), g)] = value.astype(jnp.bfloat16).reshape(
+            experts, count, slim
         )
         if m >= 2:
             fetch(0, m - 2, slot, (g,))
@@ -540,17 +544,21 @@
             pair_sum(1, *steps[step - 1])
         if step == 0:
             via_sum(0, 0)
-        if step == 4:
-            plane_sum(0, 0)
         if step == 5:
             via_sum(1, 0)
-    pair_sum(1, 1, 0)
+        if step == 6:
+            plane_sum(0, 0)
+        if step == 9:
+            via_sum(1, 1)
+            plane_sum(1, 0)
+    pair_sum(1, 2, 0)
+    via_sum(1, 2)
+    plane_sum(1, 1)
     finish(0, 0)
-    plane_sum(1, 0)
-    via_sum(1, 1)
+    plane_sum(1, 2)
     finish(1, 0)
-    plane_sum(1, 1)
     finish(1, 1)
+    finish(1, 2)
     for copies in pairs.values():
         for copy in copies:
             copy.wait_send()
@@ -605,8 +613,8 @@
             pltpu.VMEM((2, 2, experts, rows, cols // 2), bf16),
             pltpu.VMEM((2, experts - 1, rows, cols), bf16),
             pltpu.VMEM((2, rows, cols), bf16),
-            dma((3, 2, 2)),
-            dma((7,)),
+            dma((3, 2, 3)),
+            dma((9,)),
             dma((experts,)),
             dma((experts,)),
             dma((2, experts)),
@@ -615,16 +623,16 @@
             dma((2, experts, 5)),
             dma((2, experts, lanes, tensor)),
             dma((2, experts, lanes, tensor)),
-            dma((2, 2, lanes, tensor)),
-            dma((2, 2, lanes, tensor)),
-            dma((2, 2, 2, 2, experts)),
-            dma((2, 2, 2, 2, experts)),
-            dma((2, 2, 2, experts)),
-            dma((2, 2, 2, experts)),
-            dma((2, 2, experts)),
-            dma((2, 2, experts)),
-            dma((2, 2, lanes)),
-            dma((2, 2, lanes)),
+            dma((2, 3, lanes, tensor)),
+            dma((2, 3, lanes, tensor)),
+            dma((2, 3, 2, 2, experts)),
+            dma((2, 3, 2, 2, experts)),
+            dma((2, 3, 2, experts)),
+            dma((2, 3, 2, experts)),
+            dma((2, 3, experts)),
+            dma((2, 3, experts)),
+            dma((2, 3, lanes)),
+            dma((2, 3, lanes)),
         ],
         compiler_params=pltpu.CompilerParams(
             collective_id=0, has_side_effects=True, vmem_limit_bytes=62 * 1024 * 1024

time: 155 us -> 155 us (level)
  no operation moved by 1% of the time
where the time goes in v5:
time: 155 us; the launch traced here: 154 us
  Pallas kernels  147 us (95%)
  local copies, waits for them, and re-layouts  5.5 us (4%)
    pallas_call x1, Pallas kernels, local(): pl.pallas_call(functools.partial(expert_kernel, sizes), out_shape=(result...  147 us
    unnamed x2, local copies, waits for them, and re-layouts  4.13 us

profile of v5, /device:TPU:0, one launch (start us, length us, event | category | flops | bytes accessed | tf_op | source)
XLA Modules:
  0.0 154.2 jit_solution(14746343898337456625)
XLA Ops:
  0.6 0.8 slice_bitcast_fusion.1
  1.4 0.8 broadcast_subtract_fusion
  2.2 0.6 broadcast_in_dim.30.table
  2.8 147.3 %expert_layer.1 = (bf16[64,6144]{1,0:T(8,128)(2,1)}, bf16[64,6144]{1,0:T(8,128)(2,1)}) custom-call(bf16[128,6144]{1,0:T(8,128)(2,1)} %tokens.1, bf16[128,6144]{1,0:T(8,128)(2,1)} %grads.1, f32[4,8,128]{2,1,0:T(8,128)} %broadcast_in_dim.30.table, bf16[6144,1024]{1,0:T(8,128)(2,1)} %bitcast.10, bf16[6144,1024]{1,0:T(8,128)(2,1)} %bitcast.11, ...), custom_call_target="tpu_custom_call" | custom-call | flops 38654705664 | bytes 75497472 | tf_op jit(solution)/shard_map/expert_layer/pallas_call | solution.py:593
  150.1 2.1 %copy.11 = bf16[64,6144]{1,0:T(8,128)(2,1)} copy(bf16[64,6144]{1,0:T(8,128)(2,1)} %get-tuple-element.8) | data formatting | bytes 1572864
  152.1 2.1 %copy.12 = bf16[64,6144]{1,0:T(8,128)(2,1)} copy(bf16[64,6144]{1,0:T(8,128)(2,1)} %get-tuple-element.9) | data formatting | bytes 1572864
  (1 shorter events, 0.0 us)
